TPU v7x, 512 devices: a whole 4x8x8 slice. The times are simulated.
512 devices in a mesh: layer: 16 (over y, core), front: 32 (over z, x).
Axes of the slice: x: 4, y: 8, z: 8, core: 2. Of those that a mesh axis runs over, the one named last changes fastest.
Arguments:
- child_rhs: bfloat16 [16, 2, 48, 8192], P('layer', None, None, 'front'), may hold values from -6 to 6
- parent_rhs: bfloat16 [16, 2, 48, 4096], P('layer', None, None, 'front'), may hold values from -6 to 6
- root_rhs: bfloat16 [16, 2, 48, 4096], P('layer', None, None, 'front'), may hold values from -6 to 6
- child_inverse: bfloat16 [16, 2048, 8192], P('layer', None, 'front'), as said below
- child_update: bfloat16 [16, 8192, 2048], P('layer', 'front'), may hold values from -0.125 to 0.125
- parent_inverse: bfloat16 [16, 2048, 4096], P('layer', None, 'front'), as said below
- parent_update: bfloat16 [16, 4096, 3072], P('layer', 'front'), may hold values from -0.125 to 0.125
- root_inverse: bfloat16 [16, 4096, 4096], P('layer', None, 'front'), as said below
- coupling: float32 [16, 4096], P('layer', 'front'), may hold values from 0.25 to 1
- child_map: int32 [4, 2048], replicated, may hold values from 0 to 6143, as said below
- parent_map: int32 [2, 3072], replicated, may hold values from 0 to 4095, as said below
Outputs:
- solution: bfloat16 [16, 2, 48, 4096], P('layer', None, None, 'front')
Inputs may be any that keep to these rules, and one draw needn't show every extreme that they name: `child_map`: each row holds 2048 distinct entries; values below 2048 name rows of the parent front's separator, the others name row value - 2048 of the top separator. `parent_map`: each row holds 3072 distinct rows of the top separator. `child_inverse`: each group's matrix, read as rows k and columns f * 2048 + j, is zero where k > j. `parent_inverse`: each group's matrix, read as rows k and columns f * 2048 + j, is zero where k > j. `root_inverse`: each group's matrix is zero below its diagonal.
All inputs are finite; a program needn't handle non-finite values.
Results may differ from a plain program's by a relative error of at most 0.02.
Values may be sent and summed in bfloat16 or wider, within the bound.
A program may use at most 64 MiB of HBM per device.

v0:
```python
import jax
import jax.numpy as jnp
from jax import lax
from jax.sharding import PartitionSpec as P

S0 = 4096


def partner_2(value, axis, apart):
    mask = 2**apart
    pairs = [(source, source ^ mask) for source in range(lax.axis_size(axis))]
    return lax.ppermute(value, axis, pairs)


def cut_along(x, dim, count):
    dims = x.shape
    blocks = x.reshape(*dims[:dim], count, dims[dim] // count, *dims[dim + 1 :])
    return jnp.moveaxis(blocks, dim, 0)


def sent_and_summed(x, axis, dim):
    count = lax.axis_size(axis)
    blocks = lax.all_to_all(cut_along(x, dim, count), axis, 0, 0, tiled=True)
    return jnp.sum(blocks.astype(jnp.float32), axis=0)


def copy_for_each(x, axis):
    copies = jnp.broadcast_to(x, (lax.axis_size(axis), *x.shape))
    return lax.all_to_all(copies, axis, split_axis=0, concat_axis=0, tiled=True)


def joined_along(blocks, dim):
    blocks = jnp.moveaxis(blocks, 0, dim)
    dims = blocks.shape
    return blocks.reshape(*dims[:dim], dims[dim] * dims[dim + 1], *dims[dim + 2 :])


def collect_2(x, axis, dim):
    blocks = copy_for_each(x, axis)
    return joined_along(blocks, dim)


def shifted(value, axis, steps):
    count = lax.axis_size(axis)
    first, last = (max(0, -steps), min(count, count - steps))
    return lax.ppermute(value, axis, [(source, source + steps) for source in range(first, last)])


def collect(shard, share_count, level_id):
    front_index = lax.axis_index("front")
    bit_count = share_count.bit_length() - 1
    joined = shard
    for bit_pos in range(bit_count):
        if level_id == 2:
            partner = partner_2(joined, "front", bit_pos)
        else:
            partner = partner_2(joined, "front", bit_pos)
        high_bit = front_index >> bit_pos & 1 == 1
        first_piece = jnp.where(high_bit, partner, joined)
        second_piece = jnp.where(high_bit, joined, partner)
        joined = jnp.concatenate([first_piece, second_piece], 1)
    return joined


def parent_updates(own_parent, parent_shares):
    front_index = lax.axis_index("front")
    buffer = lax.optimization_barrier(own_parent.astype(jnp.bfloat16)).astype(jnp.float32)
    bit_count = parent_shares.bit_length() - 1
    for bit_pos in reversed(range(bit_count)):
        half_width = buffer.shape[1] // 2
        lower_cols = buffer[:, :half_width]
        upper_cols = buffer[:, half_width:]
        upper_side = front_index >> bit_pos & 1 == 1
        sending = jnp.where(upper_side, lower_cols, upper_cols)
        partner = partner_2(sending.astype(jnp.bfloat16), "front", bit_pos).astype(sending.dtype)
        buffer = jnp.where(upper_side, upper_cols, lower_cols) + partner
    return buffer


def lower_levels(
    child_rhs,
    parent_rhs,
    child_inverse,
    child_update,
    parent_inverse,
    parent_update,
    child_map,
    parent_map,
):
    devices = lax.axis_size("front")
    front_index = lax.axis_index("front")
    child_shares = devices // 4
    parent_shares = devices // 2
    row_count = child_rhs.shape[0]
    parent_size = parent_inverse.shape[0]
    child_full = collect(child_rhs, child_shares, 2)
    child_solved = jnp.dot(child_full, child_inverse, preferred_element_type=jnp.float32).astype(
        jnp.bfloat16
    )
    child_terms = jnp.dot(child_solved, child_update, preferred_element_type=jnp.float32)
    child_front = front_index // child_shares
    targets = child_map[child_front]
    to_parent = jnp.where(targets < parent_size, targets, parent_size)
    to_root = jnp.where(targets >= parent_size, targets - parent_size, S0)
    own_parent = (
        jnp.zeros((row_count, parent_size), jnp.float32)
        .at[:, to_parent]
        .add(child_terms, mode="drop")
    )
    root_terms = (
        jnp.zeros((row_count, S0), jnp.float32).at[:, to_root].add(child_terms, mode="drop")
    )
    summed = parent_updates(own_parent, parent_shares)
    parent_now = (parent_rhs.astype(jnp.float32) - summed).astype(jnp.bfloat16)
    parent_full = collect(parent_now, parent_shares, 1)
    parent_solved = jnp.dot(parent_full, parent_inverse, preferred_element_type=jnp.float32).astype(
        jnp.bfloat16
    )
    parent_terms = jnp.dot(parent_solved, parent_update, preferred_element_type=jnp.float32)
    parent_targets = parent_map[front_index // parent_shares]
    return root_terms.at[:, parent_targets].add(parent_terms)


def root_level(root_terms, root_rhs, incoming, root_inverse, coupling):
    front_index = lax.axis_index("front")
    share_width = root_rhs.shape[1]
    own_cols = lax.dynamic_slice_in_dim(root_terms, front_index * share_width, share_width, 1)
    own_cols = own_cols + incoming.astype(jnp.float32) - root_rhs.astype(jnp.float32)
    root_total = lax.dynamic_update_slice_in_dim(root_terms, own_cols, front_index * share_width, 1)
    share_sum = sent_and_summed(root_total.astype(jnp.bfloat16), "front", 1)
    share_now = (-share_sum).astype(jnp.bfloat16)
    root_solved = jnp.dot(
        collect_2(share_now, "front", 1), root_inverse, preferred_element_type=jnp.float32
    )
    return (
        root_solved.astype(jnp.bfloat16),
        (coupling[None, :] * root_solved).astype(jnp.bfloat16),
    )


def body(
    child_rhs,
    parent_rhs,
    root_rhs,
    child_inverse,
    child_update,
    parent_inverse,
    parent_update,
    root_inverse,
    coupling,
    child_map,
    parent_map,
):
    row_count = child_rhs.shape[2]
    stacked_terms = lower_levels(
        child_rhs[0].reshape(2 * row_count, child_rhs.shape[3]),
        parent_rhs[0].reshape(2 * row_count, parent_rhs.shape[3]),
        child_inverse[0],
        child_update[0],
        parent_inverse[0],
        parent_update[0],
        child_map,
        parent_map,
    )
    first_terms = stacked_terms[:row_count]
    second_terms = stacked_terms[row_count:]
    silent = jnp.zeros_like(root_rhs[0, 0])
    first_sol, outgoing = root_level(
        first_terms, root_rhs[0, 0], silent, root_inverse[0], coupling[0]
    )
    incoming = shifted(outgoing, "layer", 1)
    second_sol, leftover = root_level(
        second_terms, root_rhs[0, 1], incoming, root_inverse[0], coupling[0]
    )
    return jnp.stack([first_sol, second_sol], axis=0)[None]


def solution(mesh):
    placed = (
        P("layer", None, None, "front"),
        P("layer", None, None, "front"),
        P("layer", None, None, "front"),
        P("layer", None, "front"),
        P("layer", "front", None),
        P("layer", None, "front"),
        P("layer", "front", None),
        P("layer", None, "front"),
        P("layer", "front"),
        P(),
        P(),
    )
    return jax.shard_map(
        body, mesh=mesh, in_specs=placed, out_specs=P("layer", None, None, "front"), check_vma=False
    )
```

profile of v0, /device:TPU:24, one launch (start us, length us, event | category | flops | bytes accessed | tf_op | source)
XLA Modules:
  0.0 229.8 jit_solution(7260393284263410026)
XLA Ops:
  0.0 3.5 %collective-permute-start = (bf16[96,256]{1,0:T(8,128)(2,1)}, bf16[96,256]{1,0:T(8,128)(2,1)S(1)}, u32[]{:S(2)}, u32[]{:S(2)}) collective-permute-start(bf16[96,256]{1,0:T(8,128)(2,1)} %bitcast.85), channel_id=1, source_target_pairs={{0,1},{1,0},{2,3},{3,2},{4,5},{5,4},{6,7},{7,6},{8,9},{9,8},{10,11... | collective-permute-start | bytes 147464 | tf_op jit(solution)/shard_map/ppermute | solution.py:12
  3.5 2.8 %collective-permute-done = bf16[96,256]{1,0:T(8,128)(2,1)S(1)} collective-permute-done((bf16[96,256]{1,0:T(8,128)(2,1)}, bf16[96,256]{1,0:T(8,128)(2,1)S(1)}, u32[]{:S(2)}, u32[]{:S(2)}) %collective-permute-start) | collective-permute-done | bytes 49184 | tf_op jit(solution)/shard_map/ppermute | solution.py:12
  6.3 0.8 broadcast_select_fusion.11
  7.1 4.9 %collective-permute-start.1 = (bf16[96,512]{1,0:T(8,128)(2,1)S(1)}, bf16[96,512]{1,0:T(8,128)(2,1)S(1)}, u32[]{:S(2)}, u32[]{:S(2)}) collective-permute-start(bf16[96,512]{1,0:T(8,128)(2,1)S(1)} %pad_maximum_fusion.3), channel_id=1, source_target_pairs={{0,2},{1,3},{2,0},{3,1},{4,6},{5,7},{6,4},{7,5},{8,10},{9,11},{10,... | collective-permute-start | bytes 294920 | tf_op jit(solution)/shard_map/ppermute | solution.py:12
  12.1 3.1 %collective-permute-done.1 = bf16[96,512]{1,0:T(8,128)(2,1)S(1)} collective-permute-done((bf16[96,512]{1,0:T(8,128)(2,1)S(1)}, bf16[96,512]{1,0:T(8,128)(2,1)S(1)}, u32[]{:S(2)}, u32[]{:S(2)}) %collective-permute-start.1) | collective-permute-done | bytes 98336 | tf_op jit(solution)/shard_map/ppermute | solution.py:12
  15.2 4.3 %collective-permute-start.2 = (bf16[96,1024]{1,0:T(8,128)(2,1)S(1)}, bf16[96,1024]{1,0:T(8,128)(2,1)S(1)}, u32[]{:S(2)}, u32[]{:S(2)}) collective-permute-start(bf16[96,1024]{1,0:T(8,128)(2,1)S(1)} %pad_maximum_fusion.1), channel_id=1, source_target_pairs={{0,4},{1,5},{2,6},{3,7},{4,0},{5,1},{6,2},{7,3},{8,12},{9,13},{10,... | collective-permute-start | bytes 589832 | tf_op jit(solution)/shard_map/ppermute | solution.py:12
  19.5 0.8 compare_select_fusion.1
  20.3 2.8 %collective-permute-done.2 = bf16[96,1024]{1,0:T(8,128)(2,1)S(1)} collective-permute-done((bf16[96,1024]{1,0:T(8,128)(2,1)S(1)}, bf16[96,1024]{1,0:T(8,128)(2,1)S(1)}, u32[]{:S(2)}, u32[]{:S(2)}) %collective-permute-start.2) | collective-permute-done | bytes 196640 | tf_op jit(solution)/shard_map/ppermute | solution.py:12
  23.2 0.8 convolution_bitcast_fusion.1
  24.0 0.3 copy.36
  24.4 11.7 %scatter_custom_fusion.1 = f32[96,2048]{0,1:T(8,128)S(1)} fusion(s32[2048]{0:T(1024)S(1)} %bitcast.87, f32[2048,96]{1,0:T(8,128)S(1)} %copy.36, f32[]{:T(128)} %constant.18.clone.1), kind=kCustom, calls=%fused_computation.25 | custom fusion | flops 196608 | bytes 786436 | tf_op jit(solution)/shard_map/scatter-add | solution.py:108
  36.3 6.1 %collective-permute-start.3 = (bf16[96,1024]{0,1:T(8,128)(2,1)S(1)}, bf16[96,1024]{0,1:T(8,128)(2,1)S(1)}, u32[]{:S(2)}, u32[]{:S(2)}) collective-permute-start(bf16[96,1024]{0,1:T(8,128)(2,1)S(1)} %select_convert_fusion), channel_id=1, source_target_pairs={{0,8},{1,9},{2,10},{3,11},{4,12},{5,13},{6,14},{7,15},{8,0},{9,1},... | collective-permute-start | bytes 589832 | tf_op jit(solution)/shard_map/ppermute | solution.py:12
  42.4 8.7 %collective-permute-done.3 = bf16[96,1024]{0,1:T(8,128)(2,1)S(1)} collective-permute-done((bf16[96,1024]{0,1:T(8,128)(2,1)S(1)}, bf16[96,1024]{0,1:T(8,128)(2,1)S(1)}, u32[]{:S(2)}, u32[]{:S(2)}) %collective-permute-start.3) | collective-permute-done | bytes 196640 | tf_op jit(solution)/shard_map/ppermute | solution.py:12
  51.3 2.6 %collective-permute-start.4 = (bf16[96,512]{0,1:T(8,128)(2,1)S(1)}, bf16[96,512]{0,1:T(8,128)(2,1)S(1)}, u32[]{:S(2)}, u32[]{:S(2)}) collective-permute-start(bf16[96,512]{0,1:T(8,128)(2,1)S(1)} %select_convert_fusion.1), channel_id=1, source_target_pairs={{0,4},{1,5},{2,6},{3,7},{4,0},{5,1},{6,2},{7,3},{8,12},{9,13},{10,... | collective-permute-start | bytes 294920 | tf_op jit(solution)/shard_map/ppermute | solution.py:12
  53.9 4.2 %collective-permute-done.4 = bf16[96,512]{0,1:T(8,128)(2,1)S(1)} collective-permute-done((bf16[96,512]{0,1:T(8,128)(2,1)S(1)}, bf16[96,512]{0,1:T(8,128)(2,1)S(1)}, u32[]{:S(2)}, u32[]{:S(2)}) %collective-permute-start.4) | collective-permute-done | bytes 98336 | tf_op jit(solution)/shard_map/ppermute | solution.py:12
  58.2 4.9 %collective-permute-start.5 = (bf16[96,256]{0,1:T(8,128)(2,1)S(1)}, bf16[96,256]{0,1:T(8,128)(2,1)S(1)}, u32[]{:S(2)}, u32[]{:S(2)}) collective-permute-start(bf16[96,256]{0,1:T(8,128)(2,1)S(1)} %select_convert_fusion.2), channel_id=1, source_target_pairs={{0,2},{1,3},{2,0},{3,1},{4,6},{5,7},{6,4},{7,5},{8,10},{9,11},{10,... | collective-permute-start | bytes 147464 | tf_op jit(solution)/shard_map/ppermute | solution.py:12
  63.1 2.7 %collective-permute-done.5 = bf16[96,256]{0,1:T(8,128)(2,1)S(1)} collective-permute-done((bf16[96,256]{0,1:T(8,128)(2,1)S(1)}, bf16[96,256]{0,1:T(8,128)(2,1)S(1)}, u32[]{:S(2)}, u32[]{:S(2)}) %collective-permute-start.5) | collective-permute-done | bytes 49184 | tf_op jit(solution)/shard_map/ppermute | solution.py:12
  65.9 3.4 %collective-permute-start.6 = (bf16[96,128]{0,1:T(8,128)(2,1)S(1)}, bf16[96,128]{0,1:T(8,128)(2,1)S(1)}, u32[]{:S(2)}, u32[]{:S(2)}) collective-permute-start(bf16[96,128]{0,1:T(8,128)(2,1)S(1)} %select_convert_fusion.3), channel_id=1, source_target_pairs={{0,1},{1,0},{2,3},{3,2},{4,5},{5,4},{6,7},{7,6},{8,9},{9,8},{10,11... | collective-permute-start | bytes 73736 | tf_op jit(solution)/shard_map/ppermute | solution.py:12
  69.4 2.4 %collective-permute-done.6 = bf16[96,128]{0,1:T(8,128)(2,1)S(1)} collective-permute-done((bf16[96,128]{0,1:T(8,128)(2,1)S(1)}, bf16[96,128]{0,1:T(8,128)(2,1)S(1)}, u32[]{:S(2)}, u32[]{:S(2)}) %collective-permute-start.6) | collective-permute-done | bytes 24608 | tf_op jit(solution)/shard_map/ppermute | solution.py:12
  71.9 3.4 %collective-permute-start.7 = (bf16[96,128]{0,1:T(8,128)(2,1)S(1)}, bf16[96,128]{0,1:T(8,128)(2,1)S(1)}, u32[]{:S(2)}, u32[]{:S(2)}) collective-permute-start(bf16[96,128]{0,1:T(8,128)(2,1)S(1)} %subtract_convert_fusion), channel_id=1, source_target_pairs={{0,1},{1,0},{2,3},{3,2},{4,5},{5,4},{6,7},{7,6},{8,9},{9,8},{10,11... | collective-permute-start | bytes 73736 | tf_op jit(solution)/shard_map/ppermute | solution.py:12
  75.3 2.4 %collective-permute-done.7 = bf16[96,128]{0,1:T(8,128)(2,1)S(1)} collective-permute-done((bf16[96,128]{0,1:T(8,128)(2,1)S(1)}, bf16[96,128]{0,1:T(8,128)(2,1)S(1)}, u32[]{:S(2)}, u32[]{:S(2)}) %collective-permute-start.7) | collective-permute-done | bytes 24608 | tf_op jit(solution)/shard_map/ppermute | solution.py:12
  77.7 5.3 %collective-permute-start.8 = (bf16[96,256]{0,1:T(8,128)(2,1)S(1)}, bf16[96,256]{0,1:T(8,128)(2,1)S(1)}, u32[]{:S(2)}, u32[]{:S(2)}) collective-permute-start(bf16[96,256]{0,1:T(8,128)(2,1)S(1)} %pad_maximum_fusion.4), channel_id=1, source_target_pairs={{0,2},{1,3},{2,0},{3,1},{4,6},{5,7},{6,4},{7,5},{8,10},{9,11},{10,... | collective-permute-start | bytes 147464 | tf_op jit(solution)/shard_map/ppermute | solution.py:12
  83.0 2.4 %collective-permute-done.8 = bf16[96,256]{0,1:T(8,128)(2,1)S(1)} collective-permute-done((bf16[96,256]{0,1:T(8,128)(2,1)S(1)}, bf16[96,256]{0,1:T(8,128)(2,1)S(1)}, u32[]{:S(2)}, u32[]{:S(2)}) %collective-permute-start.8) | collective-permute-done | bytes 49184 | tf_op jit(solution)/shard_map/ppermute | solution.py:12
  85.5 2.7 %collective-permute-start.9 = (bf16[96,512]{0,1:T(8,128)(2,1)S(1)}, bf16[96,512]{0,1:T(8,128)(2,1)S(1)}, u32[]{:S(2)}, u32[]{:S(2)}) collective-permute-start(bf16[96,512]{0,1:T(8,128)(2,1)S(1)} %pad_maximum_fusion.2), channel_id=1, source_target_pairs={{0,4},{1,5},{2,6},{3,7},{4,0},{5,1},{6,2},{7,3},{8,12},{9,13},{10,... | collective-permute-start | bytes 294920 | tf_op jit(solution)/shard_map/ppermute | solution.py:12
  88.2 0.1 copy.49
  88.3 5.5 %collective-permute-done.9 = bf16[96,512]{0,1:T(8,128)(2,1)S(1)} collective-permute-done((bf16[96,512]{0,1:T(8,128)(2,1)S(1)}, bf16[96,512]{0,1:T(8,128)(2,1)S(1)}, u32[]{:S(2)}, u32[]{:S(2)}) %collective-permute-start.9) | collective-permute-done | bytes 98336 | tf_op jit(solution)/shard_map/ppermute | solution.py:12
  93.9 0.8 pad_maximum_fusion
  94.7 3.9 %collective-permute-start.10 = (bf16[96,1024]{0,1:T(8,128)(2,1)}, bf16[96,1024]{0,1:T(8,128)(2,1)}, u32[]{:S(2)}, u32[]{:S(2)}) collective-permute-start(bf16[96,1024]{0,1:T(8,128)(2,1)} %pad_maximum_fusion), channel_id=1, source_target_pairs={{0,8},{1,9},{2,10},{3,11},{4,12},{5,13},{6,14},{7,15},{8,0},{9,1},... | collective-permute-start | bytes 589832 | tf_op jit(solution)/shard_map/ppermute | solution.py:12
  98.6 12.3 %scatter_custom_fusion = f32[96,4096]{0,1:T(8,128)S(1)} fusion(s32[2048]{0:T(1024)S(1)} %bitcast.86, f32[2048,96]{1,0:T(8,128)} %copy-done.4, f32[]{:T(128)} %constant.18.clone.1), kind=kCustom, calls=%fused_computation.14 | custom fusion | flops 196608 | bytes 1573376 | tf_op jit(solution)/shard_map/scatter-add | solution.py:111
  111.0 1.9 broadcast_select_fusion.1
  112.8 3.1 %convolution_bitcast_fusion = f32[3072,96]{0,1:T(8,128)} fusion(bf16[1,128,3072]{2,1,0:T(8,128)(2,1)} %param.17, bf16[96,1024]{0,1:T(8,128)(2,1)} %get-tuple-element.8, bf16[96,1024]{0,1:T(8,128)(2,1)} %get-tuple-element.7, bf16[1,2048,128]{2,1,0:T(8,128)(2,1)} %param.16), kind=kOutput, calls=%fused_computation.3 | convolution fusion | flops 126627840 | bytes 2883584 | tf_op jit(solution)/shard_map/dot_general | solution.py:119
  115.9 2.9 %copy.39 = f32[3072,96]{1,0:T(8,128)} copy(f32[3072,96]{0,1:T(8,128)} %convolution_bitcast_fusion) | data formatting | bytes 2359296 | tf_op jit(solution)/shard_map/dot_general | solution.py:119
  118.8 18.0 %scatter_fusion = f32[96,4096]{0,1:T(8,128)S(1)} fusion(f32[96,4096]{0,1:T(8,128)S(1)} %scatter_custom_fusion, s32[3072]{0:T(1024)S(1)} %bitcast.84, f32[3072,96]{1,0:T(8,128)} %copy.39), kind=kCustom, calls=%fused_computation.2 | custom fusion | flops 294912 | bytes 3551232 | tf_op jit(solution)/shard_map/scatter-add | solution.py:121
  136.8 2.0 fusion.36
  138.8 0.1 convert_element_type.104
  139.0 0.4 copy.41
  139.3 23.5 %all_to_all.20 = bf16[32,48,128]{2,1,0:T(8,128)(2,1)S(1)} all-to-all(bf16[32,48,128]{2,1,0:T(8,128)(2,1)S(1)} %bitcast.83), channel_id=1, replica_groups=mesh['layer'=16,'front'=32] {'front'}, dimensions={0} | all-to-all | bytes 786432 | tf_op jit(solution)/shard_map/all_to_all | solution.py:23
  162.9 16.6 %all_to_all.21 = bf16[32,48,128]{2,1,0:T(8,128)(2,1)S(1)} all-to-all(bf16[32,48,128]{2,1,0:T(8,128)(2,1)S(1)} %broadcast_in_dim.26), channel_id=1, replica_groups=mesh['layer'=16,'front'=32] {'front'}, dimensions={0} | all-to-all | bytes 786432 | tf_op jit(solution)/shard_map/all_to_all | solution.py:29
  179.5 1.5 convert_bitcast_fusion.1
  181.0 1.9 collective-permute-start.11
  183.0 1.5 copy.50
  184.5 1.6 collective-permute-done.11
  186.1 1.4 fusion.31
  187.4 1.2 bitcast_bitcast_fusion
  188.6 20.0 %all_to_all.22 = bf16[32,48,128]{2,1,0:T(8,128)(2,1)S(1)} all-to-all(bf16[32,48,128]{2,1,0:T(8,128)(2,1)S(1)} %bitcast_bitcast_fusion), channel_id=1, replica_groups=mesh['layer'=16,'front'=32] {'front'}, dimensions={0} | all-to-all | bytes 786432 | tf_op jit(solution)/shard_map/all_to_all | solution.py:23
  208.7 20.1 %all_to_all.23 = bf16[32,48,128]{2,1,0:T(8,128)(2,1)S(1)} all-to-all(bf16[32,48,128]{2,1,0:T(8,128)(2,1)S(1)} %broadcast_in_dim.27), channel_id=1, replica_groups=mesh['layer'=16,'front'=32] {'front'}, dimensions={0} | all-to-all | bytes 786432 | tf_op jit(solution)/shard_map/all_to_all | solution.py:29
  228.8 0.3 fusion
  229.2 0.6 maximum_bitcast_fusion
  (50 shorter events, 1.1 us)
Async XLA Ops:
  0.0 23.2 %copy-start = (bf16[1,256,2048]{2,1,0:T(8,128)(2,1)S(1)}, bf16[1,256,2048]{2,1,0:T(8,128)(2,1)}, u32[]{:S(2)}) copy-start(bf16[1,256,2048]{2,1,0:T(8,128)(2,1)} %param.15) | copy-start | bytes 3145732
  0.0 23.2 %copy-start.3 = (bf16[1,2048,256]{2,1,0:T(8,128)(2,1)S(1)}, bf16[1,2048,256]{2,1,0:T(8,128)(2,1)}, u32[]{:S(2)}) copy-start(bf16[1,2048,256]{2,1,0:T(8,128)(2,1)} %param.14) | copy-start | bytes 3145732
  0.0 6.3 %collective-permute-start = (bf16[96,256]{1,0:T(8,128)(2,1)}, bf16[96,256]{1,0:T(8,128)(2,1)S(1)}, u32[]{:S(2)}, u32[]{:S(2)}) collective-permute-start(bf16[96,256]{1,0:T(8,128)(2,1)} %bitcast.85), channel_id=1, source_target_pairs={{0,1},{1,0},{2,3},{3,2},{4,5},{5,4},{6,7},{7,6},{8,9},{9,8},{10,11... | collective-permute-start | bytes 147464 | tf_op jit(solution)/shard_map/ppermute | solution.py:12
  7.1 8.0 %collective-permute-start.1 = (bf16[96,512]{1,0:T(8,128)(2,1)S(1)}, bf16[96,512]{1,0:T(8,128)(2,1)S(1)}, u32[]{:S(2)}, u32[]{:S(2)}) collective-permute-start(bf16[96,512]{1,0:T(8,128)(2,1)S(1)} %pad_maximum_fusion.3), channel_id=1, source_target_pairs={{0,2},{1,3},{2,0},{3,1},{4,6},{5,7},{6,4},{7,5},{8,10},{9,11},{10,... | collective-permute-start | bytes 294920 | tf_op jit(solution)/shard_map/ppermute | solution.py:12
  15.2 7.9 %collective-permute-start.2 = (bf16[96,1024]{1,0:T(8,128)(2,1)S(1)}, bf16[96,1024]{1,0:T(8,128)(2,1)S(1)}, u32[]{:S(2)}, u32[]{:S(2)}) collective-permute-start(bf16[96,1024]{1,0:T(8,128)(2,1)S(1)} %pad_maximum_fusion.1), channel_id=1, source_target_pairs={{0,4},{1,5},{2,6},{3,7},{4,0},{5,1},{6,2},{7,3},{8,12},{9,13},{10,... | collective-permute-start | bytes 589832 | tf_op jit(solution)/shard_map/ppermute | solution.py:12
  24.4 11.9 %copy-start.4 = (f32[2048,96]{1,0:T(8,128)}, f32[2048,96]{1,0:T(8,128)S(1)}, u32[]{:S(2)}) copy-start(f32[2048,96]{1,0:T(8,128)S(1)} %copy.36) | copy-start | bytes 2359300
  36.3 33.0 %copy-start.6 = (bf16[1,2,48,128]{3,2,1,0:T(8,128)(2,1)S(1)}, bf16[1,2,48,128]{3,2,1,0:T(8,128)(2,1)}, u32[]{:S(2)}) copy-start(bf16[1,2,48,128]{3,2,1,0:T(8,128)(2,1)} %param.12) | copy-start | bytes 73732
  36.3 14.8 %collective-permute-start.3 = (bf16[96,1024]{0,1:T(8,128)(2,1)S(1)}, bf16[96,1024]{0,1:T(8,128)(2,1)S(1)}, u32[]{:S(2)}, u32[]{:S(2)}) collective-permute-start(bf16[96,1024]{0,1:T(8,128)(2,1)S(1)} %select_convert_fusion), channel_id=1, source_target_pairs={{0,8},{1,9},{2,10},{3,11},{4,12},{5,13},{6,14},{7,15},{8,0},{9,1},... | collective-permute-start | bytes 589832 | tf_op jit(solution)/shard_map/ppermute | solution.py:12
  51.2 37.0 %slice-start = ((bf16[1,2,48,128]{3,2,1,0:T(8,128)(2,1)}), bf16[1,1,48,128]{3,2,1,0:T(8,128)(2,1)S(1)}, s32[]{:S(2)}) async-start(bf16[1,2,48,128]{3,2,1,0:T(8,128)(2,1)} %param.13), calls=%async_computation.4 | async-start | bytes 24576 | tf_op jit(solution)/shard_map/slice | solution.py:169
  51.3 47.3 %copy-start.7 = (s32[2,3072]{1,0:T(2,128)S(1)}, s32[2,3072]{1,0:T(2,128)}, u32[]{:S(2)}) copy-start(s32[2,3072]{1,0:T(2,128)} %param.21) | copy-start | bytes 73732
  51.3 6.9 %collective-permute-start.4 = (bf16[96,512]{0,1:T(8,128)(2,1)S(1)}, bf16[96,512]{0,1:T(8,128)(2,1)S(1)}, u32[]{:S(2)}, u32[]{:S(2)}) collective-permute-start(bf16[96,512]{0,1:T(8,128)(2,1)S(1)} %select_convert_fusion.1), channel_id=1, source_target_pairs={{0,4},{1,5},{2,6},{3,7},{4,0},{5,1},{6,2},{7,3},{8,12},{9,13},{10,... | collective-permute-start | bytes 294920 | tf_op jit(solution)/shard_map/ppermute | solution.py:12
  58.2 7.7 %collective-permute-start.5 = (bf16[96,256]{0,1:T(8,128)(2,1)S(1)}, bf16[96,256]{0,1:T(8,128)(2,1)S(1)}, u32[]{:S(2)}, u32[]{:S(2)}) collective-permute-start(bf16[96,256]{0,1:T(8,128)(2,1)S(1)} %select_convert_fusion.2), channel_id=1, source_target_pairs={{0,2},{1,3},{2,0},{3,1},{4,6},{5,7},{6,4},{7,5},{8,10},{9,11},{10,... | collective-permute-start | bytes 147464 | tf_op jit(solution)/shard_map/ppermute | solution.py:12
  65.9 6.0 %collective-permute-start.6 = (bf16[96,128]{0,1:T(8,128)(2,1)S(1)}, bf16[96,128]{0,1:T(8,128)(2,1)S(1)}, u32[]{:S(2)}, u32[]{:S(2)}) collective-permute-start(bf16[96,128]{0,1:T(8,128)(2,1)S(1)} %select_convert_fusion.3), channel_id=1, source_target_pairs={{0,1},{1,0},{2,3},{3,2},{4,5},{5,4},{6,7},{7,6},{8,9},{9,8},{10,11... | collective-permute-start | bytes 73736 | tf_op jit(solution)/shard_map/ppermute | solution.py:12
  71.9 5.8 %collective-permute-start.7 = (bf16[96,128]{0,1:T(8,128)(2,1)S(1)}, bf16[96,128]{0,1:T(8,128)(2,1)S(1)}, u32[]{:S(2)}, u32[]{:S(2)}) collective-permute-start(bf16[96,128]{0,1:T(8,128)(2,1)S(1)} %subtract_convert_fusion), channel_id=1, source_target_pairs={{0,1},{1,0},{2,3},{3,2},{4,5},{5,4},{6,7},{7,6},{8,9},{9,8},{10,11... | collective-permute-start | bytes 73736 | tf_op jit(solution)/shard_map/ppermute | solution.py:12
  77.7 7.7 %collective-permute-start.8 = (bf16[96,256]{0,1:T(8,128)(2,1)S(1)}, bf16[96,256]{0,1:T(8,128)(2,1)S(1)}, u32[]{:S(2)}, u32[]{:S(2)}) collective-permute-start(bf16[96,256]{0,1:T(8,128)(2,1)S(1)} %pad_maximum_fusion.4), channel_id=1, source_target_pairs={{0,2},{1,3},{2,0},{3,1},{4,6},{5,7},{6,4},{7,5},{8,10},{9,11},{10,... | collective-permute-start | bytes 147464 | tf_op jit(solution)/shard_map/ppermute | solution.py:12
  85.5 8.4 %collective-permute-start.9 = (bf16[96,512]{0,1:T(8,128)(2,1)S(1)}, bf16[96,512]{0,1:T(8,128)(2,1)S(1)}, u32[]{:S(2)}, u32[]{:S(2)}) collective-permute-start(bf16[96,512]{0,1:T(8,128)(2,1)S(1)} %pad_maximum_fusion.2), channel_id=1, source_target_pairs={{0,4},{1,5},{2,6},{3,7},{4,0},{5,1},{6,2},{7,3},{8,12},{9,13},{10,... | collective-permute-start | bytes 294920 | tf_op jit(solution)/shard_map/ppermute | solution.py:12
  94.7 16.3 %collective-permute-start.10 = (bf16[96,1024]{0,1:T(8,128)(2,1)}, bf16[96,1024]{0,1:T(8,128)(2,1)}, u32[]{:S(2)}, u32[]{:S(2)}) collective-permute-start(bf16[96,1024]{0,1:T(8,128)(2,1)} %pad_maximum_fusion), channel_id=1, source_target_pairs={{0,8},{1,9},{2,10},{3,11},{4,12},{5,13},{6,14},{7,15},{8,0},{9,1},... | collective-permute-start | bytes 589832 | tf_op jit(solution)/shard_map/ppermute | solution.py:12
  138.9 40.5 %copy-start.8 = (f32[1,128]{1,0:T(1,128)S(1)}, f32[1,128]{1,0:T(1,128)}, u32[]{:S(2)}) copy-start(f32[1,128]{1,0:T(1,128)} %param.19) | copy-start | bytes 1540
  139.3 43.6 %copy-start.1 = (f32[48,4096]{0,1:T(8,128)S(1)}, f32[48,4096]{0,1:T(8,128)}, u32[]{:S(2)}) copy-start(f32[48,4096]{0,1:T(8,128)} %get-tuple-element.6) | copy-start | bytes 2359300
  179.5 6.6 %copy-start.5 = (bf16[1,2,48,128]{3,2,1,0:T(8,128)(2,1)S(1)}, bf16[1,2,48,128]{3,2,1,0:T(8,128)(2,1)}, u32[]{:S(2)}) copy-start(bf16[1,2,48,128]{3,2,1,0:T(8,128)(2,1)} %param.13) | copy-start | bytes 73732
  181.0 5.0 %collective-permute-start.11 = (bf16[48,128]{1,0:T(8,128)(2,1)S(1)}, bf16[48,128]{1,0:T(8,128)(2,1)S(1)}, u32[]{:S(2)}, u32[]{:S(2)}) collective-permute-start(bf16[48,128]{1,0:T(8,128)(2,1)S(1)} %get-tuple-element.24), channel_id=1, source_target_pairs={{0,32},{32,64},{64,96},{96,128},{128,160},{160,192},{192,224},{224... | collective-permute-start | bytes 36872 | tf_op jit(solution)/shard_map/ppermute | solution.py:46
  184.5 44.4 %copy-start.2 = (bf16[1,4096,128]{2,1,0:T(8,128)(2,1)S(1)}, bf16[1,4096,128]{2,1,0:T(8,128)(2,1)}, u32[]{:S(2)}) copy-start(bf16[1,4096,128]{2,1,0:T(8,128)(2,1)} %param.18) | copy-start | bytes 3145732
where the time goes:
time: 231 us; the launch traced here: 230 us
  blocking collectives  80.1 us (35%)
  other arithmetic  50.4 us (22%)
  starting transfers between devices  46.9 us (20%)
  waiting for transfers between devices  38.7 us (17%)
  local copies, waits for them, and re-layouts  7.45 us (3%)
  matrix products  5.69 us (2%)
    ppermute x11, starting transfers between devices, partner_2(): return lax.ppermute(value, axis, pairs)  45 us
    all_to_all x2, blocking collectives, sent_and_summed(): blocks = lax.all_to_all(cut_along(x, dim, count), axis, 0, 0, tiled=True)  43.4 us
    ppermute x11, waiting for transfers between devices, partner_2(): return lax.ppermute(value, axis, pairs)  37.1 us
    all_to_all x2, blocking collectives, copy_for_each(): return lax.all_to_all(copies, axis, split_axis=0, concat_axis=0, tiled=True)  36.7 us
    scatter-add x1, other arithmetic, lower_levels(): return root_terms.at[:, parent_targets].add(parent_terms)  18 us
    scatter-add x1, other arithmetic, lower_levels(): jnp.zeros((row_count, S0), jnp.float32).at[:, to_root]  12.3 us
    scatter-add x1, other arithmetic, lower_levels(): own_parent = jnp.zeros((row_count, parent_size), jnp.float32).at[:, to_pa...  11.7 us
  transfers between devices with their start and end apart: 12, of which 11 were waited for; matrix products, arithmetic and copies ran while one was open for 6% of the time, Pallas kernels for 0%

commit v1 on v0

v1 whole, which is shorter than its diff:
```python
import functools

import jax
import jax.numpy as jnp
from jax import lax
from jax.experimental import pallas as pl
from jax.experimental.pallas import tpu as pltpu
from jax.sharding import PartitionSpec as P

BF = jnp.bfloat16
F32 = jnp.float32
MESH = pl.DeviceIdType.MESH

ROWS = 48
W = 128
NX, NZ = 4, 8
NF = NX * NZ
NC, NP = 8, 16
S1 = 2048
S2 = 2048
U1 = 3072
U2 = 2048
S0 = 4096
TN = 512
KC = 256


def one_hot(col_ref, k, first):
    col = col_ref[k * KC : (k + 1) * KC]
    parts = []
    for t in range(TN // W):
        lane = lax.broadcasted_iota(jnp.int32, (KC, W), 1) + (first + t * W)
        parts.append(jnp.where(lane.astype(jnp.int16) == col, BF(1), BF(0)))
    return jnp.concatenate(parts, axis=1)


def placed(rows_refs, col_ref, depth, first):
    sums = [None] * len(rows_refs)
    for k in range(depth // KC):
        hot = one_hot(col_ref, k, first)
        for m, rows in enumerate(rows_refs):
            part = jnp.dot(rows(k * KC, KC), hot, preferred_element_type=F32)
            sums[m] = part if sums[m] is None else sums[m] + part
    return sums


def joined(buf, b, count):
    return jnp.concatenate([buf[b, k] for k in range(count)], axis=1)


def kernel(
    child_rhs, parent_rhs, root_rhs, ci_h, cu_h, pi_h, pu_h, ri_h, coupling_h, cmap_h, pmap_h,
    out,
    ci, cu, pi, pu, ri, coup, cmap, pmap, prhs, rrhs,
    ccol, pcol, cup, pup, c_s, u_s, r_s, root1,
    cbuf, psend, prec, gbuf, xsend, xrec, zsend, zrec, abuf, hsend,
    lsem, csem_s, csem_r, psem_s, psem_r, gsem_s, gsem_r,
    xsem_s, xsem_r, zsem_s, zsem_r, asem_z, asem_f, asem_r,
):
    me = lax.axis_index("front")
    lay = lax.axis_index("layer")
    layers = lax.axis_size("layer")
    z, x = me // NX, me % NX
    i8, i16 = me % NC, me % NP
    b8, b16 = me - i8, me - i16
    has_next = lay < layers - 1
    has_prev = lay > 0

    barrier = pltpu.get_barrier_semaphore()

    def greet(dev):
        pl.semaphore_signal(barrier, inc=1, device_id=dev, device_id_type=MESH)

    @pl.when(has_prev)
    def _():
        @pl.loop(0, z + 1)
        def _(k):
            greet({"layer": lay - 1, "front": k * NX + x})

    for o in (4, 3, 2, 1):
        greet({"front": ((z // 4 * 4 + 4) % NZ + (z + o) % 4) * NX + x})

    @pl.loop(1, NP)
    def _(o):
        greet({"front": b16 + (i16 + o) % NP})

    loads = []

    def load(src, dst):
        copy = pltpu.make_async_copy(src, dst, lsem.at[len(loads)])
        copy.start()
        loads.append(copy)
        return copy

    l_cmap = load(cmap_h, cmap)
    l_cu = load(cu_h.at[0], cu)
    l_child = [load(child_rhs.at[0, b], cbuf.at[b, i8]) for b in range(2)]
    l_pmap = load(pmap_h, pmap)
    l_pu = load(pu_h.at[0], pu)
    l_ci = load(ci_h.at[0], ci)
    l_prhs = load(parent_rhs.at[0], prhs)
    l_pi = load(pi_h.at[0], pi)
    l_rrhs = load(root_rhs.at[0], rrhs)
    l_coup = load(coupling_h, coup)
    l_ri = load(ri_h.at[0], ri)

    @pl.loop(i8 + 1, NC)
    def _(k):
        for b in range(2):
            cbuf[b, k] = jnp.zeros((ROWS, 2 * W), BF)

    @pl.loop(i16 + 1, NP)
    def _(k):
        for b in range(2):
            gbuf[b, k] = jnp.zeros((ROWS, W), BF)

    @pl.loop((z + 1) * NX, NF)
    def _(k):
        for b in range(3):
            abuf[b, k] = jnp.zeros((ROWS, W), BF)

    @pl.when(jnp.logical_not(has_prev))
    def _():
        @pl.loop(0, (z + 1) * NX)
        def _(k):
            abuf[2, k] = jnp.zeros((ROWS, W), BF)

    def columns(map_ref, row, col_ref, count):
        for k in range(count // W):
            targets = map_ref[0:1, k * W : (k + 1) * W]
            for f in range(1, map_ref.shape[0]):
                targets = jnp.where(row == f, map_ref[f : f + 1, k * W : (k + 1) * W], targets)
            col_ref[k * W : (k + 1) * W] = jnp.broadcast_to(targets, (W, W)).T.astype(jnp.int16)

    l_cmap.wait()
    columns(cmap, me // NC, ccol, U2)
    l_cu.wait()

    @pl.loop(0, S1 // TN)
    def _(j):
        halves = [lambda k, n, h=h: cu[h * W : (h + 1) * W, k : k + n] for h in range(2)]
        for h, part in enumerate(placed(halves, ccol, U2, j * TN)):
            cup[j, h * W : (h + 1) * W] = part.astype(BF)

    l_pmap.wait()
    columns(pmap, me // NP, pcol, U1)

    for copy in l_child:
        copy.wait()
    pl.semaphore_wait(barrier, NP - 1 + 4 + jnp.where(has_next, NZ - z, 0))

    def send(src, dst, s_sem, r_sem, dev):
        return pltpu.make_async_remote_copy(
            src_ref=src, dst_ref=dst, send_sem=s_sem, recv_sem=r_sem, device_id=dev, device_id_type=MESH
        )

    def child_copy(b, to, slot):
        return send(
            cbuf.at[b, slot], cbuf.at[b, slot], csem_s.at[b, to], csem_r.at[b, slot], {"front": b8 + to}
        )

    for b in range(2):
        @pl.loop(i8 + 1, NC)
        def _(k):
            child_copy(b, k, i8).start()

    l_pu.wait()

    @pl.loop(0, NZ)
    def _(j):
        whole = [lambda k, n: pu[:, k : k + n]]
        pup[j] = placed(whole, pcol, U1, j * TN)[0].astype(BF)

    def parent_copy(b, to, slot):
        return send(
            psend.at[b, to], prec.at[b, slot], psem_s.at[b, to], psem_r.at[b, slot], {"front": b16 + to}
        )

    l_ci.wait()
    for b in range(2):
        @pl.loop(0, i8)
        def _(k):
            child_copy(b, i8, k).wait_recv()

        solved = jnp.dot(joined(cbuf, b, NC), ci[...], preferred_element_type=F32).astype(BF)
        c_s[b * ROWS : (b + 1) * ROWS] = solved
        for j in range(S1 // TN):
            terms = jnp.dot(solved, cup[j], preferred_element_type=F32).astype(BF)
            for t in range(TN // W):
                psend[b, j * (TN // W) + t] = terms[:, t * W : (t + 1) * W]

        @pl.loop(1, NP)
        def _(o):
            parent_copy(b, (i16 + o) % NP, i16).start()

    for j in range(U2 // TN):
        u_s[:, j * TN : (j + 1) * TN] = jnp.dot(
            c_s[...], cu[:, j * TN : (j + 1) * TN], preferred_element_type=F32
        ).astype(BF)

    @pl.loop(0, NZ)
    def _(j):
        whole = [lambda k, n: u_s[:, k : k + n]]
        r_s[j] = placed(whole, ccol, U2, S1 + j * TN)[0]

    def gather_copy(b, to, slot):
        return send(
            gbuf.at[b, slot], gbuf.at[b, slot], gsem_s.at[b, to], gsem_r.at[b, slot], {"front": b16 + to}
        )

    l_prhs.wait()
    for b in range(2):
        @pl.loop(1, NP)
        def _(o):
            parent_copy(b, i16, (i16 + o) % NP).wait_recv()

        prec[b, i16] = psend[b, i16]
        total = prec[b, 0].astype(F32)
        for k in range(1, NP):
            total += prec[b, k].astype(F32)
        gbuf[b, i16] = (prhs[b].astype(F32) - total).astype(BF)

        @pl.loop(i16 + 1, NP)
        def _(k):
            gather_copy(b, k, i16).start()

    def row_of(s):
        return (z + s + 2) % NZ

    def x_copy(b, half, p):
        to = (x + p) % NX
        part = pl.ds(half * 4, 4)
        return send(
            xsend.at[b, to, part], xrec.at[b, x, part],
            xsem_s.at[b, half, p], xsem_r.at[b, half, x], {"front": z * NX + to},
        )

    def x_arrival(b, half, p):
        frm = (x + p) % NX
        part = pl.ds(half * 4, 4)
        return send(
            xsend.at[b, x, part], xrec.at[b, frm, part],
            xsem_s.at[b, half, p], xsem_r.at[b, half, frm], {"front": me},
        )

    l_pi.wait()
    for b in range(2):
        @pl.loop(0, i16)
        def _(k):
            gather_copy(b, i16, k).wait_recv()

        solved = jnp.dot(joined(gbuf, b, NP), pi[...], preferred_element_type=F32).astype(BF)
        for half in range(2):
            for s in range(half * 4, half * 4 + 4):
                row = row_of(s)
                terms = jnp.dot(solved, pup[row], preferred_element_type=F32)
                terms = (terms + r_s[row, b * ROWS : (b + 1) * ROWS]).astype(BF)
                for t in range(NX):
                    xsend[b, t, s] = terms[:, t * W : (t + 1) * W]
            for p in (2, 1, 3):
                x_copy(b, half, p).start()

    def z_copy(b, s):
        row = row_of(s)
        return send(
            zsend.at[b, s], zrec.at[b, z], zsem_s.at[b, s], zsem_r.at[b, z], {"front": row * NX + x}
        )

    def sum_x(b):
        for half in range(2):
            for p in (1, 3, 2):
                x_arrival(b, half, p).wait_recv()
            for s in range(half * 4, half * 4 + 4):
                total = xsend[b, x, s].astype(F32)
                for p in (1, 2, 3):
                    total += xrec[b, (x + p) % NX, s].astype(F32)
                zsend[b, s] = total.astype(BF)
                if s != 6:
                    z_copy(b, s).start()

    def row_copy(a, o, src, dev):
        return send(src, abuf.at[a, me], asem_z.at[a, o], asem_r.at[a, me], dev)

    def row_arrival(a, o, slot):
        return send(abuf.at[a, slot], abuf.at[a, slot], asem_z.at[a, o], asem_r.at[a, slot], {"front": me})

    def pass_on(a, o, p):
        slot = me - NX * o
        return send(
            abuf.at[a, slot], abuf.at[a, slot], asem_f.at[a, NX * o + p], asem_r.at[a, slot],
            {"front": z * NX + (x + p) % NX},
        )

    def sum_z(b):
        for o in range(1, NZ):
            frm = (z + o) % NZ
            send(
                zsend.at[b, 6], zrec.at[b, frm], zsem_s.at[b, 0], zsem_r.at[b, frm], {"front": me}
            ).wait_recv()
        total = zsend[b, 6].astype(F32)
        for o in range(1, NZ):
            total += zrec[b, (z + o) % NZ].astype(F32)
        abuf[b, me] = (rrhs[b].astype(F32) - total).astype(BF)
        for o in (4, 3, 5, 2, 6, 1, 7):
            @pl.when(z + o < NZ)
            def _():
                row_copy(b, o, abuf.at[b, me], {"front": me + NX * o}).start()
        for p in (2, 1, 3):
            pass_on(b, 0, p).start()

    def pass_rows(a, offsets):
        for o in offsets:
            @pl.when(z >= o)
            def _():
                row_arrival(a, o, me - NX * o).wait_recv()
                for p in (2, 1, 3):
                    pass_on(a, o, p).start()

    def wait_passed(a):
        for o in range(NZ):
            @pl.when(z >= o)
            def _():
                for p in (1, 2, 3):
                    row_arrival(a, o, (z - o) * NX + (x + p) % NX).wait_recv()

    far = (1, 7, 2, 6, 3, 5, 4)

    def root_solve(a):
        return jnp.dot(joined(abuf, a, NF), ri[...], preferred_element_type=F32)

    l_rrhs.wait()
    sum_x(0)
    sum_z(0)
    sum_x(1)
    pass_rows(0, far)
    sum_z(1)
    l_coup.wait()
    l_ri.wait()
    wait_passed(0)
    solved = root_solve(0)
    hsend[...] = (coup[...] * solved).astype(BF)

    @pl.when(has_next)
    def _():
        for o in (4, 3, 5, 2, 6, 1, 7, 0):
            @pl.when(z + o < NZ)
            def _():
                row_copy(2, o, hsend, {"layer": lay + 1, "front": me + NX * o}).start()

    out[0, 0] = solved.astype(BF)
    pass_rows(1, far)

    @pl.when(has_prev)
    def _():
        pass_rows(2, (0,) + far)

    wait_passed(1)
    root1[...] = root_solve(1)

    @pl.when(has_prev)
    def _():
        wait_passed(2)

    out[0, 1] = (root1[...] - root_solve(2)).astype(BF)

    for b in range(2):
        @pl.loop(i8 + 1, NC)
        def _(k):
            child_copy(b, k, i8).wait_send()

        @pl.loop(1, NP)
        def _(o):
            parent_copy(b, (i16 + o) % NP, i16).wait_send()

        @pl.loop(i16 + 1, NP)
        def _(k):
            gather_copy(b, k, i16).wait_send()

        for half in range(2):
            for p in (1, 2, 3):
                x_copy(b, half, p).wait_send()
        for s in range(NZ):
            if s != 6:
                z_copy(b, s).wait_send()

        @pl.loop(1, NZ - z)
        def _(o):
            row_copy(b, o, abuf.at[b, me], {"front": me + NX * o}).wait_send()

        @pl.loop(0, z + 1)
        def _(o):
            for p in (1, 2, 3):
                pass_on(b, o, p).wait_send()

    @pl.when(has_next)
    def _():
        @pl.loop(0, NZ - z)
        def _(o):
            row_copy(2, o, hsend, {"layer": lay + 1, "front": me + NX * o}).wait_send()

    @pl.when(has_prev)
    def _():
        @pl.loop(0, z + 1)
        def _(o):
            for p in (1, 2, 3):
                pass_on(2, o, p).wait_send()


def body(*args):
    piece = (ROWS, W)
    dma = pltpu.SemaphoreType.DMA
    scratch = [
        pltpu.VMEM((S2, 256), BF), pltpu.VMEM((256, U2), BF), pltpu.VMEM((S1, W), BF),
        pltpu.VMEM((W, U1), BF), pltpu.VMEM((S0, W), BF), pltpu.VMEM((1, W), F32),
        pltpu.VMEM((4, U2), jnp.int32), pltpu.VMEM((2, U1), jnp.int32),
        pltpu.VMEM((2, *piece), BF), pltpu.VMEM((2, *piece), BF),
        pltpu.VMEM((U2, W), jnp.int16), pltpu.VMEM((U1, W), jnp.int16),
        pltpu.VMEM((S1 // TN, 256, TN), BF), pltpu.VMEM((NZ, W, TN), BF),
        pltpu.VMEM((2 * ROWS, 256), BF), pltpu.VMEM((2 * ROWS, U2), BF),
        pltpu.VMEM((NZ, 2 * ROWS, TN), F32), pltpu.VMEM(piece, F32),
        pltpu.VMEM((2, NC, ROWS, 256), BF),
        pltpu.VMEM((2, NP, *piece), BF), pltpu.VMEM((2, NP, *piece), BF), pltpu.VMEM((2, NP, *piece), BF),
        pltpu.VMEM((2, NX, NZ, *piece), BF), pltpu.VMEM((2, NX, NZ, *piece), BF),
        pltpu.VMEM((2, NZ, *piece), BF), pltpu.VMEM((2, NZ, *piece), BF),
        pltpu.VMEM((3, NF, *piece), BF), pltpu.VMEM(piece, BF),
        dma((11 + 1,)), dma((2, NC)), dma((2, NC)), dma((2, NP)), dma((2, NP)), dma((2, NP)), dma((2, NP)),
        dma((2, 2, NX)), dma((2, 2, NX)), dma((2, NZ)), dma((2, NZ)),
        dma((3, NZ)), dma((3, NF)), dma((3, NF)),
    ]
    return pl.pallas_call(
        kernel,
        out_shape=jax.ShapeDtypeStruct((1, 2, ROWS, W), BF),
        in_specs=[pl.BlockSpec(memory_space=pl.ANY)] * 11,
        out_specs=pl.BlockSpec(memory_space=pltpu.VMEM),
        scratch_shapes=scratch,
        compiler_params=pltpu.CompilerParams(
            collective_id=0, has_side_effects=True, vmem_limit_bytes=40 * 2**20
        ),
    )(*args)


def solution(mesh):
    placed_as = (
        P("layer", None, None, "front"),
        P("layer", None, None, "front"),
        P("layer", None, None, "front"),
        P("layer", None, "front"),
        P("layer", "front", None),
        P("layer", None, "front"),
        P("layer", "front", None),
        P("layer", None, "front"),
        P("layer", "front"),
        P(),
        P(),
    )
    return jax.shard_map(
        body, mesh=mesh, in_specs=placed_as, out_specs=P("layer", None, None, "front"), check_vma=False
    )
```

time: 231 us -> 80.1 us (0.35)
  the two profiles are of different devices: /device:TPU:24 before, /device:TPU:472 now
where the time goes in v1:
time: 80.1 us; the launch traced here: 79.5 us
  Pallas kernels  68.6 us (86%)
  local copies, waits for them, and re-layouts  10.9 us (14%)
    pallas_call x1, Pallas kernels, body(): pl.pallas_call(kernel, out_shape=jax.ShapeDtypeStruct((1, 2, ROWS, W), BF...  68.6 us
    unnamed x23, local copies, waits for them, and re-layouts  10.9 us

profile of v1, /device:TPU:472, one launch (start us, length us, event | category | flops | bytes accessed | tf_op | source)
XLA Modules:
  0.0 79.5 jit_solution(5445568619726002700)
XLA Ops:
  0.0 0.0 copy-start
  0.0 1.2 %copy-done = bf16[1,2048,256]{2,1,0:T(8,128)(2,1)S(1)} copy-done((bf16[1,2048,256]{2,1,0:T(8,128)(2,1)S(1)}, bf16[1,2048,256]{2,1,0:T(8,128)(2,1)}, u32[]{:S(2)}) %copy-start) | copy-done | bytes 1048600
  1.2 0.0 copy-start.1
  1.2 1.2 %copy-done.1 = bf16[1,256,2048]{2,1,0:T(8,128)(2,1)S(1)} copy-done((bf16[1,256,2048]{2,1,0:T(8,128)(2,1)S(1)}, bf16[1,256,2048]{2,1,0:T(8,128)(2,1)}, u32[]{:S(2)}) %copy-start.1) | copy-done | bytes 1048600
  2.5 0.0 copy-start.2
  2.5 1.2 %copy-done.2 = bf16[1,4096,128]{2,1,0:T(8,128)(2,1)S(1)} copy-done((bf16[1,4096,128]{2,1,0:T(8,128)(2,1)S(1)}, bf16[1,4096,128]{2,1,0:T(8,128)(2,1)}, u32[]{:S(2)}) %copy-start.2) | copy-done | bytes 1048600
  3.7 0.0 copy-start.3
  3.7 1.1 %copy-done.3 = bf16[1,128,3072]{2,1,0:T(8,128)(2,1)S(1)} copy-done((bf16[1,128,3072]{2,1,0:T(8,128)(2,1)S(1)}, bf16[1,128,3072]{2,1,0:T(8,128)(2,1)}, u32[]{:S(2)}) %copy-start.3) | copy-done | bytes 786456
  4.8 0.0 copy-start.4
  4.8 1.0 %copy-done.4 = bf16[1,2048,128]{2,1,0:T(8,128)(2,1)S(1)} copy-done((bf16[1,2048,128]{2,1,0:T(8,128)(2,1)S(1)}, bf16[1,2048,128]{2,1,0:T(8,128)(2,1)}, u32[]{:S(2)}) %copy-start.4) | copy-done | bytes 524312
  5.9 0.0 copy-start.5
  5.9 0.8 %copy-done.5 = bf16[1,2,48,256]{3,2,1,0:T(8,128)(2,1)S(1)} copy-done((bf16[1,2,48,256]{3,2,1,0:T(8,128)(2,1)S(1)}, bf16[1,2,48,256]{3,2,1,0:T(8,128)(2,1)}, u32[]{:S(2)}) %copy-start.5) | copy-done | bytes 49176
  6.7 0.0 copy-start.6
  6.7 0.8 copy-done.6
  7.4 0.0 copy-start.7
  7.4 0.7 copy-done.7
  8.1 0.0 copy-start.8
  8.1 0.7 copy-done.8
  8.9 0.0 copy-start.9
  8.9 0.7 copy-done.9
  9.6 0.0 copy-start.10
  9.6 0.7 copy-done.10
  10.3 68.6 %shard_map.109 = bf16[1,2,48,128]{3,2,1,0:T(8,128)(2,1)S(1)} custom-call(bf16[1,2,48,256]{3,2,1,0:T(8,128)(2,1)S(1)} %copy-done.5, bf16[1,2,48,128]{3,2,1,0:T(8,128)(2,1)S(1)} %copy-done.7, bf16[1,2,48,128]{3,2,1,0:T(8,128)(2,1)S(1)} %copy-done.8, bf16[1,2048,256]{2,1,0:T(8,128)(2,1)S(1)} %copy-done, bf16[1,256,2048]{2,1,0:T(8,128)(2,1)S(1)} %copy-done.1, ...), custom_call_target="tpu_custom_call" | custom-call | tf_op jit(solution)/shard_map/pallas_call | solution.py:430
  78.9 0.6 copy.13
Async XLA Ops:
  0.0 1.2 %copy-start = (bf16[1,2048,256]{2,1,0:T(8,128)(2,1)S(1)}, bf16[1,2048,256]{2,1,0:T(8,128)(2,1)}, u32[]{:S(2)}) copy-start(bf16[1,2048,256]{2,1,0:T(8,128)(2,1)} %ci_h.1) | copy-start | bytes 3145732
  1.2 1.2 %copy-start.1 = (bf16[1,256,2048]{2,1,0:T(8,128)(2,1)S(1)}, bf16[1,256,2048]{2,1,0:T(8,128)(2,1)}, u32[]{:S(2)}) copy-start(bf16[1,256,2048]{2,1,0:T(8,128)(2,1)} %cu_h.1) | copy-start | bytes 3145732
  2.5 1.2 %copy-start.2 = (bf16[1,4096,128]{2,1,0:T(8,128)(2,1)S(1)}, bf16[1,4096,128]{2,1,0:T(8,128)(2,1)}, u32[]{:S(2)}) copy-start(bf16[1,4096,128]{2,1,0:T(8,128)(2,1)} %ri_h.1) | copy-start | bytes 3145732
  3.7 1.1 %copy-start.3 = (bf16[1,128,3072]{2,1,0:T(8,128)(2,1)S(1)}, bf16[1,128,3072]{2,1,0:T(8,128)(2,1)}, u32[]{:S(2)}) copy-start(bf16[1,128,3072]{2,1,0:T(8,128)(2,1)} %pu_h.1) | copy-start | bytes 2359300
  4.8 1.0 %copy-start.4 = (bf16[1,2048,128]{2,1,0:T(8,128)(2,1)S(1)}, bf16[1,2048,128]{2,1,0:T(8,128)(2,1)}, u32[]{:S(2)}) copy-start(bf16[1,2048,128]{2,1,0:T(8,128)(2,1)} %pi_h.1) | copy-start | bytes 1572868
  5.9 0.8 %copy-start.5 = (bf16[1,2,48,256]{3,2,1,0:T(8,128)(2,1)S(1)}, bf16[1,2,48,256]{3,2,1,0:T(8,128)(2,1)}, u32[]{:S(2)}) copy-start(bf16[1,2,48,256]{3,2,1,0:T(8,128)(2,1)} %child_rhs.1) | copy-start | bytes 147460
  6.7 0.8 copy-start.6
  7.4 0.7 copy-start.7
  8.1 0.7 copy-start.8
  8.9 0.7 copy-start.9
  9.6 0.7 copy-start.10
